TPU v7x, 32 devices: a whole 2x2x4 slice. The times are simulated.
32 devices in a mesh: rep: 4 (over y, x), shard: 8 (over z, core).
Axes of the slice: x: 2, y: 2, z: 4, core: 2. Of those that a mesh axis runs over, the one named last changes fastest.
Arguments:
- local_dense: float32 [4, 1024, 1024], P('rep', 'shard'), may hold values from -6 to 6
- anchor_dense: float32 [1024, 1024], P('shard'), may hold values from -6 to 6
- momentum_dense: float32 [1024, 1024], P('shard'), may hold values from -6 to 6
- local_emb: float32 [4, 8192, 2048], P('rep', 'shard'), may hold values from -24 to 24
- anchor_emb: float32 [8192, 2048], P('shard'), may hold values from -24 to 24
- momentum_emb: float32 [8192, 2048], P('shard'), may hold values from -6 to 6
- proj_basis: float32 [2048, 64], P('shard'), may hold values from -6 to 6
Outputs:
- new_dense_anchor: float32 [1024, 1024], P('shard')
- new_dense_momentum: float32 [1024, 1024], P('shard')
- dense_weights: bfloat16 [1024, 1024], replicated
- new_emb_anchor: float32 [8192, 2048], P('shard')
- new_emb_momentum: float32 [8192, 2048], P('shard')
All inputs are finite; a program needn't handle non-finite values.
Results may differ from a plain program's by a relative error of at most 0.0004.
Values may be sent and summed in bfloat16 or wider, within the bound.
A program may use at most 128 MiB of HBM per device.

v0:
```python
import jax
import jax.numpy as jnp
from jax import lax
from jax.sharding import PartitionSpec as P

outer_rate = 0.7
momentum_rate = 0.9
highest = lax.Precision.HIGHEST


def dense_update(dense_sum, anchor_dense, momentum_dense, group_count):
    dense_grad = dense_sum / group_count
    dense_mom = momentum_rate * momentum_dense + dense_grad
    dense_new = anchor_dense - outer_rate * (dense_grad + momentum_rate * dense_mom)
    gathered = lax.all_gather(dense_new.astype(jnp.bfloat16), "shard", axis=0, tiled=True)
    return (dense_new, dense_mom, gathered)


def on_device(
    local_dense, anchor_dense, momentum_dense, local_emb, anchor_emb, momentum_emb, proj_basis
):
    group_count = lax.axis_size("rep")
    full_basis = lax.all_gather(proj_basis, "shard", axis=0, tiled=True)
    dense_diff = anchor_dense - local_dense[0]
    emb_diff = anchor_emb - local_emb[0]
    part_factor = jnp.dot(
        emb_diff, full_basis, precision=highest, preferred_element_type=jnp.float32
    )
    dense_sum, factor = lax.psum((dense_diff, part_factor), "rep")
    dense_new, dense_mom, gathered = dense_update(
        dense_sum, anchor_dense, momentum_dense, group_count
    )
    local_gram = lax.dot_general(
        factor,
        factor,
        (((0,), (0,)), ((), ())),
        precision=highest,
        preferred_element_type=jnp.float32,
    )
    gram_matrix = lax.psum(local_gram, "shard")
    chol_lower = jnp.linalg.cholesky(gram_matrix)
    ortho_rows = jax.scipy.linalg.solve_triangular(chol_lower, factor.T, lower=True).T
    coeff_share = lax.psum_scatter(
        lax.dot_general(
            emb_diff,
            ortho_rows,
            (((0,), (0,)), ((), ())),
            precision=highest,
            preferred_element_type=jnp.float32,
        ),
        "shard",
        scatter_dimension=0,
        tiled=True,
    )
    coeff_share = lax.psum(coeff_share, "rep")
    coefficients = lax.all_gather(coeff_share, "shard", axis=0, tiled=True)
    emb_grad = (
        lax.dot_general(
            ortho_rows,
            coefficients,
            (((1,), (1,)), ((), ())),
            precision=highest,
            preferred_element_type=jnp.float32,
        )
        / group_count
    )
    emb_mom = momentum_rate * momentum_emb + emb_grad
    emb_new = anchor_emb - outer_rate * (emb_grad + momentum_rate * emb_mom)
    return (dense_new, dense_mom, gathered, emb_new, emb_mom)


def solution(mesh):
    placed = (
        P("rep", "shard", None),
        P("shard", None),
        P("shard", None),
        P("rep", "shard", None),
        P("shard", None),
        P("shard", None),
        P("shard", None),
    )
    return jax.shard_map(
        on_device,
        mesh=mesh,
        in_specs=placed,
        out_specs=(P("shard", None), P("shard", None), P(), P("shard", None), P("shard", None)),
        check_vma=False,
    )
```

profile of v0, /device:TPU:0, one launch (start us, length us, event | category | flops | bytes accessed | tf_op | source)
XLA Modules:
  0.0 270.5 jit_solution(2345077583079396937)
XLA Ops:
  7.2 0.0 all-reduce.4.cloned.1.call-start
  7.2 16.8 %all_gather.10 = f32[2048,64]{0,1:T(8,128)S(1)} all-gather(f32[256,64]{0,1:T(8,128)} %param.13), channel_id=1, replica_groups=mesh['rep'=4,'shard'=8] {'shard'}, dimensions={0}, use_global_device_ids=true | all-gather | bytes 589824 | tf_op jit(solution)/shard_map/all_gather | solution.py:23
  24.0 12.6 %fusion.1 = f32[1024,64]{0,1:T(8,128)} fusion(f32[2048,64]{0,1:T(8,128)S(1)} %all_gather.10, f32[1024,2048]{1,0:T(8,128)} %param.11, f32[1,1024,2048]{2,1,0:T(8,128)} %param.10), kind=kOutput, calls=%fused_computation.4 | convolution fusion | flops 1612709888 | bytes 17563648 | tf_op jit(solution)/shard_map/dot_general | solution.py:26
  36.6 0.0 all-reduce.4.cloned.1.call-update
  36.6 0.0 reduce-scatter.2.cloned.1.call-start
  36.7 44.1 %all-reduce.4.cloned.1.call-done = f32[1024,64]{0,1:T(8,128)} async-done(((f32[1024,64]{0,1:T(8,128)}), f32[1024,64]{0,1:T(8,128)}) %all-reduce.4.cloned.1.call-update) | async-done | bytes 262160 | tf_op jit(solution)/shard_map/psum | solution.py:29
  80.8 1.4 fusion.7
  82.2 28.2 %psum.30 = f32[64,64]{0,1:T(8,128)S(1)} all-reduce(f32[64,64]{0,1:T(8,128)S(1)} %fusion.7), channel_id=1, replica_groups=mesh['rep'=4,'shard'=8] {'shard'}, use_global_device_ids=true, to_apply=%region_2.0 | all-reduce | flops 4096 | bytes 32768 | tf_op jit(solution)/shard_map/psum | solution.py:40
  110.3 0.1 copy.13
  110.4 5.8 %cholesky.16 = f32[64,64]{1,0:T(8,128)S(1)} custom-call(f32[64,64]{1,0:T(8,128)S(1)} %fusion.5), custom_call_target="Cholesky" | custom-call | tf_op jit(solution)/shard_map/jit(cholesky)/cholesky | solution.py:41
  116.3 0.6 compare_reduce_fusion
  116.9 0.7 fusion.2
  117.6 4.9 %custom-call.7 = f32[1,64,64]{1,2,0:T(8,128)S(1)} custom-call(f32[1,64,64]{2,1,0:T(8,128)S(1)} %fusion.2), custom_call_target="InvertDiagBlocksLowerTriangular" | custom-call | tf_op jit(solution)/shard_map/jit(_solve_triangular)/triangular_solve | solution.py:42
  122.5 1.4 fusion.3
  123.9 0.0 copy-start
  123.9 0.0 copy-start.1
  123.9 0.0 copy-start.2
  123.9 17.9 %fusion = f32[2048,64]{1,0:T(8,128)} fusion(f32[64,1024]{1,0:T(8,128)S(1)} %fusion.3, f32[1024,2048]{1,0:T(8,128)} %param.11, f32[1,1024,2048]{2,1,0:T(8,128)} %param.10), kind=kOutput, calls=%fused_computation.3 | convolution fusion | flops 1612709888 | bytes 17563648 | tf_op jit(solution)/shard_map/dot_general | solution.py:44
  141.9 0.0 reduce-scatter.2.cloned.1.call-update
  141.9 0.0 all-reduce.6.cloned.1.call-start
  141.9 0.0 copy-done
  141.9 0.0 copy-done.1
  142.0 0.9 bitcast_subtract_fusion.3
  142.8 28.8 %reduce-scatter.2.cloned.1.call-done = f32[256,64]{1,0:T(8,128)} async-done(((f32[2048,64]{1,0:T(8,128)}), f32[256,64]{1,0:T(8,128)}) %reduce-scatter.2.cloned.1.call-update) | async-done | bytes 65552 | tf_op jit(solution)/shard_map/reduce_scatter | solution.py:43
  171.6 0.0 all-reduce.6.cloned.1.call-update
  171.6 0.0 all-gather.2.cloned.1.call-start
  171.6 49.2 %all-reduce.6.cloned.1.call-done = (f32[128,1024]{1,0:T(8,128)}, f32[256,64]{1,0:T(8,128)}) async-done(((f32[128,1024]{1,0:T(8,128)}, f32[256,64]{1,0:T(8,128)}), (f32[128,1024]{1,0:T(8,128)}, f32[256,64]{1,0:T(8,128)})) %all-reduce.6.cloned.1.call-update) | async-done | bytes 589840 | tf_op jit(solution)/shard_map/psum | solution.py:29
  220.9 0.0 copy-done.2
  220.9 2.3 fusion.6
  223.1 0.0 all-gather.2.cloned.1.call-update
  223.1 22.0 %all_gather.11 = f32[2048,64]{1,0:T(8,128)S(1)} all-gather(f32[256,64]{1,0:T(8,128)} %get-tuple-element.6), channel_id=1, replica_groups=mesh['rep'=4,'shard'=8] {'shard'}, dimensions={0}, use_global_device_ids=true | all-gather | bytes 589824 | tf_op jit(solution)/shard_map/all_gather | solution.py:56
  245.2 15.7 %multiply_subtract_fusion = (f32[1024,2048]{1,0:T(8,128)}, f32[1024,2048]{1,0:T(8,128)}) fusion(f32[1024,2048]{1,0:T(8,128)} %param.11, f32[1024,2048]{1,0:T(8,128)} %param.12, f32[64,1024]{1,0:T(8,128)S(1)} %fusion.3, f32[2048,64]{1,0:T(8,128)S(1)} %all_gather.11), kind=kOutput, calls=%fused_computation.1 | convolution fusion | flops 1625292800 | bytes 34340864 | tf_op jit(solution)/shard_map/dot_general | solution.py:58
  260.9 0.0 all-gather.2.cloned.1.call-done
  260.9 3.1 %copy.19 = bf16[1024,1024]{1,0:T(8,128)(2,1)} copy(bf16[1024,1024]{1,0:T(8,128)(2,1)} %all-gather.2.cloned.1.call-done) | data formatting | bytes 4194304
  (2 shorter events, 0.0 us)
Async XLA Ops:
  7.2 73.6 %all-reduce.4.cloned.1.call-start = ((), (), s32[]{:S(2)}) async-start(), calls=%async_computation.2 | async-start | bytes 524288 | tf_op jit(solution)/shard_map/psum | solution.py:29
  36.6 134.9 %reduce-scatter.2.cloned.1.call-start = ((), (), s32[]{:S(2)}) async-start(), calls=%async_computation.3 | async-start | bytes 1179648 | tf_op jit(solution)/shard_map/reduce_scatter | solution.py:43
  123.9 18.1 %copy-start = (f32[128,1024]{1,0:T(8,128)S(1)}, f32[128,1024]{1,0:T(8,128)}, u32[]{:S(2)}) copy-start(f32[128,1024]{1,0:T(8,128)} %param.8) | copy-start | bytes 1572868
  123.9 18.1 %copy-start.1 = (f32[1,128,1024]{2,1,0:T(8,128)S(1)}, f32[1,128,1024]{2,1,0:T(8,128)}, u32[]{:S(2)}) copy-start(f32[1,128,1024]{2,1,0:T(8,128)} %param.7) | copy-start | bytes 1572868
  123.9 97.0 %copy-start.2 = (f32[128,1024]{1,0:T(8,128)S(1)}, f32[128,1024]{1,0:T(8,128)}, u32[]{:S(2)}) copy-start(f32[128,1024]{1,0:T(8,128)} %param.9) | copy-start | bytes 1572868
  141.9 79.0 %all-reduce.6.cloned.1.call-start = ((), (), s32[]{:S(2)}) async-start(), calls=%async_computation.4 | async-start | bytes 1310720 | tf_op jit(solution)/shard_map/psum | solution.py:29
  171.6 89.3 %all-gather.2.cloned.1.call-start = ((), (), s32[]{:S(2)}) async-start(), calls=%async_computation.1 | async-start | bytes 2359296 | tf_op jit(solution)/shard_map/all_gather | solution.py:15
Sparse Core Ops, SparseCore 0:
  36.7 43.9 all-reduce.3
  142.0 29.5 reduce-scatter.1
  175.5 45.3 all-reduce.5
  223.3 33.0 all-gather.1
where the time goes:
time: 271 us; the launch traced here: 270 us
  waiting for transfers between devices  122 us (45%)
  blocking collectives  67 us (25%)
  matrix products  49 us (18%)
  other arithmetic  15.2 us (6%)
  between operations  13.8 us (5%)
  local copies, waits for them, and re-layouts  3.17 us (1%)
    psum x2, waiting for transfers between devices, on_device(): dense_sum, factor = lax.psum((dense_diff, part_factor), 'rep')  93.3 us
    reduce_scatter x1, waiting for transfers between devices, on_device(): lax.psum_scatter(lax.dot_general(emb_diff, ortho_rows, (((0,), (0,)), (()...  28.8 us
    psum x1, blocking collectives, on_device(): gram_matrix = lax.psum(local_gram, 'shard')  28.2 us
    all_gather x1, blocking collectives, on_device(): coefficients = lax.all_gather(coeff_share, 'shard', axis=0, tiled=True)  22 us
    dot_general x1, matrix products, on_device(): lax.dot_general(emb_diff, ortho_rows, (((0,), (0,)), ((), ())), precision...  17.9 us
    all_gather x1, blocking collectives, on_device(): full_basis = lax.all_gather(proj_basis, 'shard', axis=0, tiled=True)  16.8 us
    dot_general x1, matrix products, on_device(): lax.dot_general(ortho_rows, coefficients, (((1,), (1,)), ((), ())), preci...  15.7 us
    dot_general x1, matrix products, on_device(): jnp.dot(emb_diff, full_basis, precision=highest, preferred_element_type=j...  12.6 us
  transfers between devices with their start and end apart: 4, of which 3 were waited for; matrix products, arithmetic and copies ran while one was open for 6% of the time, Pallas kernels for 0%

commit v1 on v0

--- a/solution.py
+++ b/solution.py
@@ -37,7 +37,7 @@
         precision=highest,
         preferred_element_type=jnp.float32,
     )
-    gram_matrix = lax.psum(local_gram, "shard")
+    gram_matrix = jnp.sum(lax.all_gather(local_gram, "shard"), axis=0)
     chol_lower = jnp.linalg.cholesky(gram_matrix)
     ortho_rows = jax.scipy.linalg.solve_triangular(chol_lower, factor.T, lower=True).T
     coeff_share = lax.psum_scatter(

time: 271 us -> 260 us (0.959)
  blocking collectives: 67 us -> 53.3 us
  waiting for transfers between devices: 122 us -> 125 us
    psum x1 -> x0, blocking collectives: 28.2 us -> none  [on_device(): gram_matrix = lax.psum(local_gram, 'shard')]
    all_gather x0 -> x1, blocking collectives: none -> 14.4 us  [on_device(): gram_matrix = jnp.sum(lax.all_gather(local_gram, 'shard'), axis=0)]
    reduce_scatter x1, waiting for transfers between devices: 28.8 us -> 31.6 us  [on_device(): lax.psum_scatter(lax.dot_general(emb_diff, ortho_rows, (((0,), (0,)), (()...]
where the time goes in v1:
time: 260 us
  waiting for transfers between devices  125 us (48%)
  blocking collectives  53.3 us (20%)
  matrix products  49 us (19%)
  other arithmetic  15.2 us (6%)
  between operations  13.8 us (5%)
  local copies, waits for them, and re-layouts  3.17 us (1%)
    psum x2, waiting for transfers between devices, on_device(): dense_sum, factor = lax.psum((dense_diff, part_factor), 'rep')  93.3 us
    reduce_scatter x1, waiting for transfers between devices, on_device(): lax.psum_scatter(lax.dot_general(emb_diff, ortho_rows, (((0,), (0,)), (()...  31.6 us
    all_gather x1, blocking collectives, on_device(): coefficients = lax.all_gather(coeff_share, 'shard', axis=0, tiled=True)  22 us
    dot_general x1, matrix products, on_device(): lax.dot_general(emb_diff, ortho_rows, (((0,), (0,)), ((), ())), precision...  17.9 us
    all_gather x1, blocking collectives, on_device(): full_basis = lax.all_gather(proj_basis, 'shard', axis=0, tiled=True)  16.8 us
    dot_general x1, matrix products, on_device(): lax.dot_general(ortho_rows, coefficients, (((1,), (1,)), ((), ())), preci...  15.7 us
    all_gather x1, blocking collectives, on_device(): gram_matrix = jnp.sum(lax.all_gather(local_gram, 'shard'), axis=0)  14.4 us
    dot_general x1, matrix products, on_device(): jnp.dot(emb_diff, full_basis, precision=highest, preferred_element_type=j...  12.6 us
  transfers between devices with their start and end apart: 4, of which 3 were waited for; matrix products, arithmetic and copies ran while one was open for 6% of the time, Pallas kernels for 0%

profile of v1, /device:TPU:0, one launch (start us, length us, event | category | flops | bytes accessed | tf_op | source)
XLA Modules:
  0.0 259.6 jit_solution(11226497604541571713)
XLA Ops:
  7.2 0.0 all-reduce.4.cloned.1.call-start
  7.2 16.8 %all_gather.16 = f32[2048,64]{0,1:T(8,128)S(1)} all-gather(f32[256,64]{0,1:T(8,128)} %param.13), channel_id=1, replica_groups=mesh['rep'=4,'shard'=8] {'shard'}, dimensions={0}, use_global_device_ids=true | all-gather | bytes 589824 | tf_op jit(solution)/shard_map/all_gather | solution.py:23
  24.0 12.6 %fusion.1 = f32[1024,64]{0,1:T(8,128)} fusion(f32[2048,64]{0,1:T(8,128)S(1)} %all_gather.16, f32[1024,2048]{1,0:T(8,128)} %param.11, f32[1,1024,2048]{2,1,0:T(8,128)} %param.10), kind=kOutput, calls=%fused_computation.4 | convolution fusion | flops 1612709888 | bytes 17563648 | tf_op jit(solution)/shard_map/dot_general | solution.py:26
  36.6 0.0 all-reduce.4.cloned.1.call-update
  36.6 0.0 reduce-scatter.2.cloned.1.call-start
  36.7 44.1 %all-reduce.4.cloned.1.call-done = f32[1024,64]{0,1:T(8,128)} async-done(((f32[1024,64]{0,1:T(8,128)}), f32[1024,64]{0,1:T(8,128)}) %all-reduce.4.cloned.1.call-update) | async-done | bytes 262160 | tf_op jit(solution)/shard_map/psum | solution.py:29
  80.8 1.4 fusion.7
  82.2 14.4 %all-gather = f32[512,64]{1,0:T(8,128)S(1)} all-gather(f32[64,64]{1,0:T(8,128)S(1)} %fusion.7), channel_id=2, replica_groups=mesh['rep'=4,'shard'=8] {'shard'}, dimensions={0}, use_global_device_ids=true | all-gather | bytes 147456 | tf_op jit(solution)/shard_map/all_gather | solution.py:40
  96.6 0.1 copy.13
  96.7 5.8 %cholesky.16 = f32[64,64]{1,0:T(8,128)S(1)} custom-call(f32[64,64]{1,0:T(8,128)S(1)} %fusion.5), custom_call_target="Cholesky" | custom-call | tf_op jit(solution)/shard_map/jit(cholesky)/cholesky | solution.py:41
  102.6 0.6 compare_reduce_fusion
  103.2 0.7 fusion.2
  103.9 4.9 %custom-call.7 = f32[1,64,64]{1,2,0:T(8,128)S(1)} custom-call(f32[1,64,64]{2,1,0:T(8,128)S(1)} %fusion.2), custom_call_target="InvertDiagBlocksLowerTriangular" | custom-call | tf_op jit(solution)/shard_map/jit(_solve_triangular)/triangular_solve | solution.py:42
  108.8 1.4 fusion.3
  110.2 0.0 copy-start
  110.2 0.0 copy-start.1
  110.2 0.0 copy-start.2
  110.2 17.9 %fusion = f32[2048,64]{1,0:T(8,128)} fusion(f32[64,1024]{1,0:T(8,128)S(1)} %fusion.3, f32[1024,2048]{1,0:T(8,128)} %param.11, f32[1,1024,2048]{2,1,0:T(8,128)} %param.10), kind=kOutput, calls=%fused_computation.3 | convolution fusion | flops 1612709888 | bytes 17563648 | tf_op jit(solution)/shard_map/dot_general | solution.py:44
  128.2 0.0 reduce-scatter.2.cloned.1.call-update
  128.2 0.0 all-reduce.6.cloned.1.call-start
  128.2 0.0 copy-done
  128.2 0.0 copy-done.1
  128.3 0.9 bitcast_subtract_fusion.3
  129.1 31.6 %reduce-scatter.2.cloned.1.call-done = f32[256,64]{1,0:T(8,128)} async-done(((f32[2048,64]{1,0:T(8,128)}), f32[256,64]{1,0:T(8,128)}) %reduce-scatter.2.cloned.1.call-update) | async-done | bytes 65552 | tf_op jit(solution)/shard_map/reduce_scatter | solution.py:43
  160.7 0.0 all-reduce.6.cloned.1.call-update
  160.7 0.0 all-gather.3.cloned.1.call-start
  160.8 49.2 %all-reduce.6.cloned.1.call-done = (f32[128,1024]{1,0:T(8,128)}, f32[256,64]{1,0:T(8,128)}) async-done(((f32[128,1024]{1,0:T(8,128)}, f32[256,64]{1,0:T(8,128)}), (f32[128,1024]{1,0:T(8,128)}, f32[256,64]{1,0:T(8,128)})) %all-reduce.6.cloned.1.call-update) | async-done | bytes 589840 | tf_op jit(solution)/shard_map/psum | solution.py:29
  210.0 0.0 copy-done.2
  210.0 2.3 fusion.6
  212.2 0.0 all-gather.3.cloned.1.call-update
  212.3 22.0 %all_gather.19 = f32[2048,64]{1,0:T(8,128)S(1)} all-gather(f32[256,64]{1,0:T(8,128)} %get-tuple-element.6), channel_id=1, replica_groups=mesh['rep'=4,'shard'=8] {'shard'}, dimensions={0}, use_global_device_ids=true | all-gather | bytes 589824 | tf_op jit(solution)/shard_map/all_gather | solution.py:56
  234.3 15.7 %multiply_subtract_fusion = (f32[1024,2048]{1,0:T(8,128)}, f32[1024,2048]{1,0:T(8,128)}) fusion(f32[1024,2048]{1,0:T(8,128)} %param.11, f32[1024,2048]{1,0:T(8,128)} %param.12, f32[64,1024]{1,0:T(8,128)S(1)} %fusion.3, f32[2048,64]{1,0:T(8,128)S(1)} %all_gather.19), kind=kOutput, calls=%fused_computation.1 | convolution fusion | flops 1625292800 | bytes 34340864 | tf_op jit(solution)/shard_map/dot_general | solution.py:58
  250.0 0.0 all-gather.3.cloned.1.call-done
  250.0 3.1 %copy.18 = bf16[1024,1024]{1,0:T(8,128)(2,1)} copy(bf16[1024,1024]{1,0:T(8,128)(2,1)} %all-gather.3.cloned.1.call-done) | data formatting | bytes 4194304
  (3 shorter events, 0.1 us)
Async XLA Ops:
  7.2 73.6 %all-reduce.4.cloned.1.call-start = ((), (), s32[]{:S(2)}) async-start(), calls=%async_computation.2 | async-start | bytes 524288 | tf_op jit(solution)/shard_map/psum | solution.py:29
  36.6 124.1 %reduce-scatter.2.cloned.1.call-start = ((), (), s32[]{:S(2)}) async-start(), calls=%async_computation.3 | async-start | bytes 1179648 | tf_op jit(solution)/shard_map/reduce_scatter | solution.py:43
  110.2 18.1 %copy-start = (f32[128,1024]{1,0:T(8,128)S(1)}, f32[128,1024]{1,0:T(8,128)}, u32[]{:S(2)}) copy-start(f32[128,1024]{1,0:T(8,128)} %param.8) | copy-start | bytes 1572868
  110.2 18.1 %copy-start.1 = (f32[1,128,1024]{2,1,0:T(8,128)S(1)}, f32[1,128,1024]{2,1,0:T(8,128)}, u32[]{:S(2)}) copy-start(f32[1,128,1024]{2,1,0:T(8,128)} %param.7) | copy-start | bytes 1572868
  110.2 99.8 %copy-start.2 = (f32[128,1024]{1,0:T(8,128)S(1)}, f32[128,1024]{1,0:T(8,128)}, u32[]{:S(2)}) copy-start(f32[128,1024]{1,0:T(8,128)} %param.9) | copy-start | bytes 1572868
  128.2 81.8 %all-reduce.6.cloned.1.call-start = ((), (), s32[]{:S(2)}) async-start(), calls=%async_computation.4 | async-start | bytes 1310720 | tf_op jit(solution)/shard_map/psum | solution.py:29
  160.7 89.3 %all-gather.3.cloned.1.call-start = ((), (), s32[]{:S(2)}) async-start(), calls=%async_computation.1 | async-start | bytes 2359296 | tf_op jit(solution)/shard_map/all_gather | solution.py:15
Sparse Core Ops, SparseCore 0:
  36.7 43.9 all-reduce.3
  128.3 32.3 reduce-scatter.1
  164.6 45.3 all-reduce.5
  212.4 33.0 all-gather.2
